TPU v7x, 32 devices: a whole 2x2x4 slice. The times are simulated.
32 devices in a mesh: groups: 2 (over x), dp: 8 (over z, y), tensor: 2 (over core).
Axes of the slice: x: 2, y: 2, z: 4, core: 2. Of those that a mesh axis runs over, the one named last changes fastest.
Arguments:
- pre_act: bfloat16 [32, 256, 13824], P(('groups', 'dp'), None, 'tensor'), parts along dimension 0, may hold values from -6 to 6
- out_grad: bfloat16 [32, 256, 5120], P(('groups', 'dp'), None, 'tensor'), parts along dimension 0, may hold values from -6 to 6
- counts: int32 [32], P(('groups', 'dp')), parts along dimension 0, may hold values from 1 to 256
- proj_in: bfloat16 [13824, 64], P('tensor'), may hold values from -0.0546875 to 0.0546875
- proj_out: bfloat16 [5120, 64], P('tensor'), may hold values from -0.078125 to 0.078125
- query_grads: bfloat16 [512, 4096], P(('dp', 'tensor')), may hold values from -0.09375 to 0.09375
Outputs:
- scores: float32 [32, 512], P('groups', ('dp', 'tensor')), parts along dimension 0
There are 2 independent parts, one for each index of `groups`. A program takes and returns all parts, laid end to end along the dimension named above; an argument that names none is the same for every part. Nothing has to cross between parts.
All inputs are finite; a program needn't handle non-finite values.
Results may differ from a plain program's by a relative error of at most 0.0042.
Values may be sent and summed in bfloat16 or wider, within the bound.
A program may use at most 64 MiB of HBM per device.

v0:
```python
import jax
import jax.numpy as jnp
from jax import lax
from jax.sharding import PartitionSpec as P


def normalized(joined, valid, rank):
    seq = joined.shape[1]
    out_proj = joined[:, :, :rank]
    in_proj = joined[:, :, rank:]
    keep = (jnp.arange(seq, dtype=jnp.int32)[None, :] < valid[:, None])[:, :, None]
    out_proj = jnp.where(keep, out_proj, jnp.zeros_like(out_proj))
    grad = jnp.einsum("esi,esj->eij", out_proj, in_proj, precision=lax.Precision.HIGHEST)
    scale = jnp.sqrt(jnp.mean(grad * grad, axis=(1, 2)) + 1e-06)
    flat = grad / scale[:, None, None]
    return flat.reshape(grad.shape[0], rank * rank).astype(jnp.bfloat16)


def shards(pre_act, out_grad, counts, proj_in, proj_out, query_grads):
    rank = proj_in.shape[1]
    act = jax.nn.gelu(pre_act.astype(jnp.float32)).astype(jnp.bfloat16)
    in_proj = jnp.einsum("esf,fr->esr", act, proj_in, preferred_element_type=jnp.float32)
    out_proj = jnp.einsum("esd,dr->esr", out_grad, proj_out, preferred_element_type=jnp.float32)
    partial_sums = jnp.concatenate([out_proj, in_proj], axis=2)
    joined = lax.psum(partial_sums, "tensor")
    flat = normalized(joined, counts, rank)
    return lax.dot_general(
        lax.all_gather(flat, "dp", axis=0, tiled=True),
        query_grads,
        (((1,), (1,)), ((), ())),
        preferred_element_type=jnp.float32,
    )


def solution(mesh):
    return jax.shard_map(
        shards,
        mesh=mesh,
        in_specs=(
            P(("groups", "dp"), None, "tensor"),
            P(("groups", "dp"), None, "tensor"),
            P(("groups", "dp")),
            P("tensor", None),
            P("tensor", None),
            P(("dp", "tensor"), None),
        ),
        out_specs=P("groups", ("dp", "tensor")),
        check_vma=False,
    )
```

profile of v0, /device:TPU:0, one launch (start us, length us, event | category | flops | bytes accessed | tf_op | source)
XLA Modules:
  0.0 77.0 jit_solution(4884693599986938812)
XLA Ops:
  6.5 0.0 copy-start
  6.5 0.0 copy-start.1
  6.5 0.0 copy-start.3
  6.5 0.0 copy-start.2
  6.5 0.0 all-reduce.2.cloned.1.call-start
  6.6 7.5 %fusion.6 = f32[2,256,64]{1,2,0:T(8,128)S(1)} fusion(bf16[2,256,6912]{2,1,0:T(8,128)(2,1)} %param.6, bf16[6912,64]{0,1:T(8,128)(2,1)} %param.9), kind=kOutput, calls=%fused_computation.10 | convolution fusion | flops 488374272 | bytes 8093696 | tf_op jit(solution)/shard_map/esf,fr->esr/dot_general | solution.py:22
  14.1 0.0 copy-done
  14.1 0.0 copy-done.1
  14.1 0.9 %fusion.9 = f32[2,256,64]{1,2,0:T(8,128)S(1)} fusion(bf16[2,256,2560]{2,1,0:T(8,128)(2,1)S(1)} %copy-done, bf16[2560,64]{0,1:T(8,128)(2,1)S(1)} %copy-done.1), kind=kOutput, calls=%fused_computation.12 | convolution fusion | flops 167772160 | bytes 3080192 | tf_op jit(solution)/shard_map/esd,dr->esr/dot_general | solution.py:23
  15.0 0.7 pad_maximum_fusion
  15.8 0.0 all-reduce.2.cloned.1.call-update
  15.8 0.0 copy-done.3
  15.8 0.1 iota_compare_fusion
  15.9 21.0 %all-reduce.2.cloned.1.call-done = f32[2,256,128]{1,2,0:T(8,128)} async-done(((f32[2,256,128]{1,2,0:T(8,128)}), f32[2,256,128]{1,2,0:T(8,128)}) %all-reduce.2.cloned.1.call-update) | async-done | bytes 262160 | tf_op jit(solution)/shard_map/psum | solution.py:25
  36.9 1.3 %multiply_reduce_fusion = (f32[2]{0:T(128)S(1)}, f32[2,64,64]{2,1,0:T(8,128)S(1)}) fusion(f32[2,256,128]{1,2,0:T(8,128)} %all-reduce.2.cloned.1.call-done, pred[2,256]{1,0:T(4,128)(4,1)S(1)} %iota_compare_fusion), kind=kOutput, calls=%fused_computation.19 | convolution fusion | flops 25214974 | bytes 295432 | tf_op jit(solution)/shard_map/esi,esj->eij/dot_general | solution.py:13
  38.2 0.1 divide_convert_fusion
  38.3 0.1 reshape.28
  38.4 30.8 %all-gather = bf16[8,2,4096]{2,1,0:T(2,128)(2,1)S(1)} all-gather(bf16[1,2,4096]{2,1,0:T(2,128)(2,1)S(1)} %reshape.28), channel_id=1, replica_groups=mesh['groups'=2,'dp'=8,'tensor'=2] {'dp'}, dimensions={0}, use_global_device_ids=true | all-gather | bytes 147456 | tf_op jit(solution)/shard_map/all_gather | solution.py:28
  69.3 0.1 reshape.29
  69.3 0.0 copy-done.2
  69.3 0.8 %fusion.20 = f32[16,32]{1,0:T(8,128)} fusion(bf16[16,4096]{1,0:T(8,128)(2,1)S(1)} %reshape.29, bf16[32,4096]{1,0:T(8,128)(2,1)S(1)} %copy-done.2), kind=kOutput, calls=%fused_computation.29 | convolution fusion | flops 4194304 | bytes 395264 | tf_op jit(solution)/shard_map/dot_general | solution.py:27
  (1 shorter events, 0.0 us)
Async XLA Ops:
  6.5 7.6 %copy-start = (bf16[2,256,2560]{2,1,0:T(8,128)(2,1)S(1)}, bf16[2,256,2560]{2,1,0:T(8,128)(2,1)}, u32[]{:S(2)}) copy-start(bf16[2,256,2560]{2,1,0:T(8,128)(2,1)} %param.7) | copy-start | bytes 7864324
  6.5 7.6 %copy-start.1 = (bf16[2560,64]{0,1:T(8,128)(2,1)S(1)}, bf16[2560,64]{0,1:T(8,128)(2,1)}, u32[]{:S(2)}) copy-start(bf16[2560,64]{0,1:T(8,128)(2,1)} %param.10) | copy-start | bytes 983044
  6.5 9.3 %copy-start.3 = (s32[2]{0:T(128)S(1)}, s32[2]{0:T(128)}, u32[]{:S(2)}) copy-start(s32[2]{0:T(128)} %param.8) | copy-start | bytes 28
  6.5 62.8 %copy-start.2 = (bf16[32,4096]{1,0:T(8,128)(2,1)S(1)}, bf16[32,4096]{1,0:T(8,128)(2,1)}, u32[]{:S(2)}) copy-start(bf16[32,4096]{1,0:T(8,128)(2,1)} %param.11) | copy-start | bytes 786436
  6.5 30.3 %all-reduce.2.cloned.1.call-start = ((), (), s32[]{:S(2)}) async-start(), calls=%async_computation | async-start | bytes 524288 | tf_op jit(solution)/shard_map/psum | solution.py:25
Sparse Core Ops, SparseCore 0:
  15.9 20.9 all-reduce.1
where the time goes:
time: 77.1 us; the launch traced here: 77 us
  blocking collectives  30.8 us (40%)
  waiting for transfers between devices  21 us (27%)
  between operations  13.4 us (17%)
  matrix products  10.5 us (14%)
  other arithmetic  0.9 us (1%)
    all_gather x1, blocking collectives, shards(): lax.all_gather(flat, 'dp', axis=0, tiled=True)  30.8 us
    psum x1, waiting for transfers between devices, shards(): joined = lax.psum(partial_sums, 'tensor')  21 us
    dot_general x1, matrix products, shards(): jnp.einsum('esf,fr->esr', act, proj_in, preferred_element_type=jnp.float32)  7.52 us
  transfers between devices with their start and end apart: 1, of which 1 were waited for; matrix products, arithmetic and copies ran while one was open for 0% of the time, Pallas kernels for 0%

commit v1 on v0

v1 whole, which is shorter than its diff:
```python
import functools
import math

import jax
import jax.numpy as jnp
from jax import lax
from jax.experimental import pallas as pl
from jax.experimental.pallas import tpu as pltpu
from jax.sharding import PartitionSpec as P

MESH = pl.DeviceIdType.MESH
NT = (((1,), (1,)), ((), ()))
TN = (((0,), (0,)), ((), ()))
C1 = math.sqrt(2.0 / math.pi)
C2 = C1 * 0.044715


def pieces(size, target):
    step = next(s for s in range(target, 0, -128) if size % s == 0)
    return [(start, step) for start in range(0, size, step)]


def gelu(x):
    x = x.astype(jnp.float32)
    half = 0.5 * x
    return (half + half * jnp.tanh(x * (C1 + C2 * (x * x)))).astype(jnp.bfloat16)


def kernel(
    nd,
    counts,
    pre,
    og,
    wi,
    wo,
    q,
    out,
    x_buf,
    g_buf,
    wi_buf,
    wo_buf,
    q_buf,
    part,
    part_in,
    grad_buf,
    flat,
    rows,
    score,
    score_in,
    x_sem,
    g_sem,
    wi_sem,
    wo_sem,
    q_sem,
    pair_send,
    pair_recv,
    ring_send,
    ring_recv,
):
    group, me, core = lax.axis_index("groups"), lax.axis_index("dp"), lax.axis_index("tensor")
    other = 1 - core
    sibling = (group, me, other)
    rank = wi.shape[0]
    seq, hidden = pre.shape[1:]
    width = og.shape[2]
    nq = q.shape[0]
    x_pieces, g_pieces = pieces(hidden, 768), pieces(width, 1280)
    example = (other, core)

    def x_copy(slot, p):
        start, size = x_pieces[p]
        cols = pl.ds(start, size)
        return pltpu.make_async_copy(pre.at[example[slot], :, cols], x_buf.at[slot, :, cols], x_sem.at[slot, p])

    def g_copy(slot, p):
        start, size = g_pieces[p]
        cols = pl.ds(start, size)
        return pltpu.make_async_copy(og.at[example[slot], :, cols], g_buf.at[slot, :, cols], g_sem.at[slot, p])

    def wi_copy(p):
        start, size = x_pieces[p]
        cols = pl.ds(start, size)
        return pltpu.make_async_copy(wi.at[:, cols], wi_buf.at[:, cols], wi_sem.at[p])

    wo_copy = pltpu.make_async_copy(wo, wo_buf, wo_sem)
    q_copy = pltpu.make_async_copy(q, q_buf.at[pl.ds(0, nq)], q_sem)
    for p in range(len(x_pieces)):
        wi_copy(p).start()
        x_copy(0, p).start()
    wo_copy.start()
    for p in range(len(g_pieces)):
        g_copy(0, p).start()
    q_copy.start()
    for p in range(len(x_pieces)):
        x_copy(1, p).start()
    for p in range(len(g_pieces)):
        g_copy(1, p).start()

    barrier = pltpu.get_barrier_semaphore()
    pl.semaphore_signal(barrier, inc=1, device_id=sibling, device_id_type=MESH)
    for k in range(1, nd):
        pl.semaphore_signal(barrier, inc=1, device_id=(group, lax.rem(me + k, nd), core), device_id_type=MESH)

    def projections(slot):
        total = jnp.zeros((seq, rank), jnp.float32)
        for p, (start, size) in enumerate(x_pieces):
            if slot == 0:
                wi_copy(p).wait()
            x_copy(slot, p).wait()
            for at in range(start, start + size, 256):
                act = gelu(x_buf[slot, :, at : at + 256])
                total += lax.dot_general(act, wi_buf[:, at : at + 256], NT, preferred_element_type=jnp.float32)
        if slot == 0:
            wo_copy.wait()
        outs = jnp.zeros((seq, rank), jnp.float32)
        for p, (start, size) in enumerate(g_pieces):
            g_copy(slot, p).wait()
            outs += lax.dot_general(
                g_buf[slot, :, start : start + size],
                wo_buf[:, start : start + size],
                NT,
                preferred_element_type=jnp.float32,
            )
        return jnp.concatenate([outs, total], axis=1)

    part[...] = projections(0)
    pl.semaphore_wait(barrier, nd)
    part_copy = pltpu.make_async_remote_copy(
        part, part_in, pair_send.at[0], pair_recv.at[0], device_id=sibling, device_id_type=MESH
    )
    part_copy.start()
    q_copy.wait()
    query_copy = pltpu.make_async_remote_copy(
        q_buf.at[pl.ds(0, nq)],
        q_buf.at[pl.ds(nq, nq)],
        pair_send.at[1],
        pair_recv.at[1],
        device_id=sibling,
        device_id_type=MESH,
    )
    query_copy.start()

    own = projections(1)
    part_copy.wait()
    keep = lax.broadcasted_iota(jnp.int32, (seq, 2 * rank), 0) < counts[core]
    joined = jnp.where(keep, own + part_in[...], 0.0)
    gram = lax.dot_general(
        joined, joined, TN, precision=lax.Precision.HIGHEST, preferred_element_type=jnp.float32
    )[:rank]
    upper = lax.broadcasted_iota(jnp.int32, (rank, 2 * rank), 1) >= rank
    grad = jnp.where(upper, gram, pltpu.roll(gram, rank, 1))
    inverse = lax.rsqrt(jnp.sum(grad * grad) / (2 * rank * rank) + 1e-06)
    grad_buf[...] = grad * inverse
    half = rank // 2
    even, odd = grad_buf[pl.ds(0, half, stride=2), :], grad_buf[pl.ds(1, half, stride=2), :]
    flat[me] = jnp.where(upper[:half], odd, even).astype(jnp.bfloat16)

    def ring_copy(k):
        return pltpu.make_async_remote_copy(
            flat.at[me],
            flat.at[me],
            ring_send.at[k],
            ring_recv.at[k],
            device_id=(group, lax.rem(me + k, nd), core),
            device_id_type=MESH,
        )

    for k in range(1, nd):
        ring_copy(k).start()
    query_copy.wait()
    for k in range(1, nd):
        came = flat.at[lax.rem(me + nd - k, nd)]
        pltpu.make_async_remote_copy(
            came,
            came,
            ring_send.at[k],
            ring_recv.at[k],
            device_id=(group, lax.rem(me + k, nd), core),
            device_id_type=MESH,
        ).wait_recv()
    rows[...] = flat[...].astype(jnp.float32).reshape(nd * half, 2 * rank)
    flats = jnp.concatenate([rows[pl.ds(a, nd, stride=half), :] for a in range(half)], axis=1).astype(jnp.bfloat16)
    result = lax.dot_general(flats, q_buf[...], NT, preferred_element_type=jnp.float32)
    score[...] = result
    score_copy = pltpu.make_async_remote_copy(
        score, score_in, pair_send.at[2], pair_recv.at[2], device_id=sibling, device_id_type=MESH
    )
    score_copy.start()
    for k in range(1, nd):
        ring_copy(k).wait_send()
    score_copy.wait()
    mine, theirs = result[:, :nq], score_in[...][:, nq:]
    out[pl.ds(0, nd, stride=2), :] = jnp.where(core == 0, mine, theirs)
    out[pl.ds(1, nd, stride=2), :] = jnp.where(core == 0, theirs, mine)


def shards(nd, pre_act, out_grad, counts, proj_in, proj_out, query_grads):
    examples, seq, hidden = pre_act.shape
    width = out_grad.shape[2]
    rank = proj_in.shape[1]
    nq, flat = query_grads.shape
    assert examples == 2 and flat == rank * rank
    any_space = pl.BlockSpec(memory_space=pltpu.HBM)
    n_x, n_g = len(pieces(hidden, 768)), len(pieces(width, 1280))
    dma = pltpu.SemaphoreType.DMA
    return pl.pallas_call(
        functools.partial(kernel, nd),
        out_shape=jax.ShapeDtypeStruct((nd * examples, nq), jnp.float32),
        in_specs=[pl.BlockSpec(memory_space=pltpu.SMEM)] + [any_space] * 5,
        out_specs=pl.BlockSpec(memory_space=pltpu.VMEM),
        scratch_shapes=[
            pltpu.VMEM((2, seq, hidden), jnp.bfloat16),
            pltpu.VMEM((2, seq, width), jnp.bfloat16),
            pltpu.VMEM((rank, hidden), jnp.bfloat16),
            pltpu.VMEM((rank, width), jnp.bfloat16),
            pltpu.VMEM((2 * nq, flat), jnp.bfloat16),
            pltpu.VMEM((seq, 2 * rank), jnp.float32),
            pltpu.VMEM((seq, 2 * rank), jnp.float32),
            pltpu.VMEM((rank, 2 * rank), jnp.float32),
            pltpu.VMEM((nd, rank // 2, 2 * rank), jnp.bfloat16),
            pltpu.VMEM((nd * rank // 2, 2 * rank), jnp.float32),
            pltpu.VMEM((nd, 2 * nq), jnp.float32),
            pltpu.VMEM((nd, 2 * nq), jnp.float32),
            dma((2, n_x)),
            dma((2, n_g)),
            dma((n_x,)),
            dma,
            dma,
            dma((3,)),
            dma((3,)),
            dma((nd,)),
            dma((nd,)),
        ],
        compiler_params=pltpu.CompilerParams(
            collective_id=0, has_side_effects=True, vmem_limit_bytes=63 * 1024 * 1024
        ),
        cost_estimate=pl.CostEstimate(
            flops=4 * seq * (hidden + width) * rank,
            bytes_accessed=4 * seq * (hidden + width),
            transcendentals=2 * seq * hidden,
        ),
    )(counts, pre_act, out_grad, proj_in.T, proj_out.T, query_grads)


def solution(mesh):
    assert mesh.shape["tensor"] == 2
    return jax.shard_map(
        functools.partial(shards, mesh.shape["dp"]),
        mesh=mesh,
        in_specs=(
            P(("groups", "dp"), None, "tensor"),
            P(("groups", "dp"), None, "tensor"),
            P(("groups", "dp")),
            P("tensor", None),
            P("tensor", None),
            P(("dp", "tensor"), None),
        ),
        out_specs=P("groups", ("dp", "tensor")),
        check_vma=False,
    )
```

time: 77.1 us -> 21.4 us (0.28)
  blocking collectives: 30.8 us -> 0 us
  waiting for transfers between devices: 21 us -> 0 us
  Pallas kernels: 0 us -> 19.9 us
  between operations: 13.4 us -> 0.01 us
  matrix products: 10.5 us -> 0 us
  local copies, waits for them, and re-layouts: 0.18 us -> 1.3 us
  other arithmetic: 0.9 us -> 0 us
    all_gather x1 -> x0, blocking collectives: 30.8 us -> none  [shards(): lax.all_gather(flat, 'dp', axis=0, tiled=True)]
    psum x1 -> x0, waiting for transfers between devices: 21 us -> none  [shards(): joined = lax.psum(partial_sums, 'tensor')]
    pallas_call x0 -> x1, Pallas kernels: none -> 19.9 us  [shards(): pl.pallas_call(functools.partial(kernel, nd), out_shape=jax.ShapeDtypeStr...]
    dot_general x4 -> x0, matrix products: 10.5 us -> none  [the longest x1 7.52 us: shards(): jnp.einsum('esf,fr->esr', act, proj_in, preferred_element_type=jnp.float32)]
    unnamed x10 -> x1, local copies, waits for them, and re-layouts: 0.18 us -> 1.3 us
  transfers between devices with their start and end apart: 1 -> 0, of which waited for: 1 -> 0; matrix products, arithmetic and copies ran while one was open for 0% -> 0% of each run, Pallas kernels for 0% -> 0%
where the time goes in v1:
time: 21.4 us; the launch traced here: 21.2 us
  Pallas kernels  19.9 us (93%)
  local copies, waits for them, and re-layouts  1.3 us (6%)
    pallas_call x1, Pallas kernels, shards(): pl.pallas_call(functools.partial(kernel, nd), out_shape=jax.ShapeDtypeStr...  19.9 us
    unnamed x1, local copies, waits for them, and re-layouts  1.3 us

profile of v1, /device:TPU:0, one launch (start us, length us, event | category | flops | bytes accessed | tf_op | source)
XLA Modules:
  0.0 21.2 jit_solution(15351918751459529274)
XLA Ops:
  0.0 19.9 %shard_map.64 = f32[16,32]{1,0:T(8,128)} custom-call(s32[2]{0:T(128)} %counts.1, bf16[2,256,6912]{2,1,0:T(8,128)(2,1)} %pre.1, bf16[2,256,2560]{2,1,0:T(8,128)(2,1)} %og.1, bf16[64,6912]{1,0:T(8,128)(2,1)} %bitcast.2, bf16[64,2560]{1,0:T(8,128)(2,1)} %bitcast.3, bf16[32,4096]{1,0:T(8,128)(2,1)} %q.1), custom_call_target="tpu_custom_call" | custom-call | flops 620756992 | bytes 9699328 | tf_op jit(solution)/shard_map/pallas_call | solution.py:206
  19.9 1.3 %copy.8 = f32[16,32]{1,0:T(8,128)} copy(f32[16,32]{1,0:T(8,128)} %shard_map.64) | data formatting | bytes 4096

commit v2 on v1

--- a/solution.py
+++ b/solution.py
@@ -11,6 +11,7 @@
 MESH = pl.DeviceIdType.MESH
 NT = (((1,), (1,)), ((), ()))
 TN = (((0,), (0,)), ((), ()))
+AHEAD = 8
 C1 = math.sqrt(2.0 / math.pi)
 C2 = C1 * 0.044715
 
@@ -64,7 +65,7 @@
     seq, hidden = pre.shape[1:]
     width = og.shape[2]
     nq = q.shape[0]
-    x_pieces, g_pieces = pieces(hidden, 768), pieces(width, 1280)
+    x_pieces, g_pieces = pieces(hidden, 2304), pieces(width, 1280)
     example = (other, core)
 
     def x_copy(slot, p):
@@ -82,19 +83,27 @@
         cols = pl.ds(start, size)
         return pltpu.make_async_copy(wi.at[:, cols], wi_buf.at[:, cols], wi_sem.at[p])
 
-    wo_copy = pltpu.make_async_copy(wo, wo_buf, wo_sem)
-    q_copy = pltpu.make_async_copy(q, q_buf.at[pl.ds(0, nq)], q_sem)
+    loads = {}
     for p in range(len(x_pieces)):
-        wi_copy(p).start()
-        x_copy(0, p).start()
-    wo_copy.start()
+        loads["wi", p] = wi_copy(p)
+        loads["x0", p] = x_copy(0, p)
+    loads["wo"] = pltpu.make_async_copy(wo, wo_buf, wo_sem)
     for p in range(len(g_pieces)):
-        g_copy(0, p).start()
-    q_copy.start()
+        loads["g0", p] = g_copy(0, p)
+    loads["q"] = pltpu.make_async_copy(q, q_buf.at[pl.ds(0, nq)], q_sem)
     for p in range(len(x_pieces)):
-        x_copy(1, p).start()
+        loads["x1", p] = x_copy(1, p)
     for p in range(len(g_pieces)):
-        g_copy(1, p).start()
+        loads["g1", p] = g_copy(1, p)
+    queue = list(loads.values())
+
+    def ready(*name):
+        loads[name if len(name) > 1 else name[0]].wait()
+        if queue:
+            queue.pop(0).start()
+
+    for _ in range(AHEAD):
+        queue.pop(0).start()
 
     barrier = pltpu.get_barrier_semaphore()
     pl.semaphore_signal(barrier, inc=1, device_id=sibling, device_id_type=MESH)
@@ -105,16 +114,16 @@
         total = jnp.zeros((seq, rank), jnp.float32)
         for p, (start, size) in enumerate(x_pieces):
             if slot == 0:
-                wi_copy(p).wait()
-            x_copy(slot, p).wait()
+                ready("wi", p)
+            ready(f"x{slot}", p)
             for at in range(start, start + size, 256):
                 act = gelu(x_buf[slot, :, at : at + 256])
                 total += lax.dot_general(act, wi_buf[:, at : at + 256], NT, preferred_element_type=jnp.float32)
         if slot == 0:
-            wo_copy.wait()
+            ready("wo")
         outs = jnp.zeros((seq, rank), jnp.float32)
         for p, (start, size) in enumerate(g_pieces):
-            g_copy(slot, p).wait()
+            ready(f"g{slot}", p)
             outs += lax.dot_general(
                 g_buf[slot, :, start : start + size],
                 wo_buf[:, start : start + size],
@@ -129,7 +138,7 @@
         part, part_in, pair_send.at[0], pair_recv.at[0], device_id=sibling, device_id_type=MESH
     )
     part_copy.start()
-    q_copy.wait()
+    ready("q")
     query_copy = pltpu.make_async_remote_copy(
         q_buf.at[pl.ds(0, nq)],
         q_buf.at[pl.ds(nq, nq)],
@@ -180,16 +189,16 @@
         ).wait_recv()
     rows[...] = flat[...].astype(jnp.float32).reshape(nd * half, 2 * rank)
     flats = jnp.concatenate([rows[pl.ds(a, nd, stride=half), :] for a in range(half)], axis=1).astype(jnp.bfloat16)
-    result = lax.dot_general(flats, q_buf[...], NT, preferred_element_type=jnp.float32)
-    score[...] = result
+    score[...] = lax.dot_general(flats, q_buf[nq:, :], NT, preferred_element_type=jnp.float32)
     score_copy = pltpu.make_async_remote_copy(
         score, score_in, pair_send.at[2], pair_recv.at[2], device_id=sibling, device_id_type=MESH
     )
     score_copy.start()
+    mine = lax.dot_general(flats, q_buf[:nq, :], NT, preferred_element_type=jnp.float32)
     for k in range(1, nd):
         ring_copy(k).wait_send()
     score_copy.wait()
-    mine, theirs = result[:, :nq], score_in[...][:, nq:]
+    theirs = score_in[...]
     out[pl.ds(0, nd, stride=2), :] = jnp.where(core == 0, mine, theirs)
     out[pl.ds(1, nd, stride=2), :] = jnp.where(core == 0, theirs, mine)
 
@@ -201,7 +210,7 @@
     nq, flat = query_grads.shape
     assert examples == 2 and flat == rank * rank
     any_space = pl.BlockSpec(memory_space=pltpu.HBM)
-    n_x, n_g = len(pieces(hidden, 768)), len(pieces(width, 1280))
+    n_x, n_g = len(pieces(hidden, 2304)), len(pieces(width, 1280))
     dma = pltpu.SemaphoreType.DMA
     return pl.pallas_call(
         functools.partial(kernel, nd),
@@ -219,8 +228,8 @@
             pltpu.VMEM((rank, 2 * rank), jnp.float32),
             pltpu.VMEM((nd, rank // 2, 2 * rank), jnp.bfloat16),
             pltpu.VMEM((nd * rank // 2, 2 * rank), jnp.float32),
-            pltpu.VMEM((nd, 2 * nq), jnp.float32),
-            pltpu.VMEM((nd, 2 * nq), jnp.float32),
+            pltpu.VMEM((nd, nq), jnp.float32),
+            pltpu.VMEM((nd, nq), jnp.float32),
             dma((2, n_x)),
             dma((2, n_g)),
             dma((n_x,)),

time: 21.4 us -> 20.2 us (0.944)
  Pallas kernels: 19.9 us -> 18.7 us
    pallas_call x1, Pallas kernels: 19.9 us -> 18.7 us  [shards(): pl.pallas_call(functools.partial(kernel, nd), out_shape=jax.ShapeDtypeStr...]
where the time goes in v2:
time: 20.2 us; the launch traced here: 20 us
  Pallas kernels  18.7 us (93%)
  local copies, waits for them, and re-layouts  1.3 us (6%)
    pallas_call x1, Pallas kernels, shards(): pl.pallas_call(functools.partial(kernel, nd), out_shape=jax.ShapeDtypeStr...  18.7 us
    unnamed x1, local copies, waits for them, and re-layouts  1.3 us

profile of v2, /device:TPU:0, one launch (start us, length us, event | category | flops | bytes accessed | tf_op | source)
XLA Modules:
  0.0 20.0 jit_solution(15776717668788709665)
XLA Ops:
  0.0 18.7 %shard_map.64 = f32[16,32]{1,0:T(8,128)} custom-call(s32[2]{0:T(128)} %counts.1, bf16[2,256,6912]{2,1,0:T(8,128)(2,1)} %pre.1, bf16[2,256,2560]{2,1,0:T(8,128)(2,1)} %og.1, bf16[64,6912]{1,0:T(8,128)(2,1)} %bitcast.2, bf16[64,2560]{1,0:T(8,128)(2,1)} %bitcast.3, bf16[32,4096]{1,0:T(8,128)(2,1)} %q.1), custom_call_target="tpu_custom_call" | custom-call | flops 620756992 | bytes 9699328 | tf_op jit(solution)/shard_map/pallas_call | solution.py:215
  18.7 1.3 %copy.8 = f32[16,32]{1,0:T(8,128)} copy(f32[16,32]{1,0:T(8,128)} %shard_map.64) | data formatting | bytes 4096

commit v3 on v2

--- a/solution.py
+++ b/solution.py
@@ -19,6 +19,13 @@
 def pieces(size, target):
     step = next(s for s in range(target, 0, -128) if size % s == 0)
     return [(start, step) for start in range(0, size, step)]
+
+
+def ramp(size):
+    units = pieces(size, 768)
+    step, n = units[0][1], len(units)
+    cuts = sorted({min(c, n) for c in (1, 5)} | {0, n})
+    return [(step * a, step * (b - a)) for a, b in zip(cuts, cuts[1:])]
 
 
 def gelu(x):
@@ -65,7 +72,7 @@
     seq, hidden = pre.shape[1:]
     width = og.shape[2]
     nq = q.shape[0]
-    x_pieces, g_pieces = pieces(hidden, 2304), pieces(width, 1280)
+    x_pieces, g_pieces = ramp(hidden), pieces(width, 1280)
     example = (other, core)
 
     def x_copy(slot, p):
@@ -210,7 +217,7 @@
     nq, flat = query_grads.shape
     assert examples == 2 and flat == rank * rank
     any_space = pl.BlockSpec(memory_space=pltpu.HBM)
-    n_x, n_g = len(pieces(hidden, 2304)), len(pieces(width, 1280))
+    n_x, n_g = len(ramp(hidden)), len(pieces(width, 1280))
     dma = pltpu.SemaphoreType.DMA
     return pl.pallas_call(
         functools.partial(kernel, nd),

time: 20.2 us -> 20.2 us (level)
  no operation moved by 1% of the time
where the time goes in v3:
time: 20.2 us; the launch traced here: 20 us
  Pallas kernels  18.7 us (93%)
  local copies, waits for them, and re-layouts  1.3 us (6%)
    pallas_call x1, Pallas kernels, shards(): pl.pallas_call(functools.partial(kernel, nd), out_shape=jax.ShapeDtypeStr...  18.7 us
    unnamed x1, local copies, waits for them, and re-layouts  1.3 us

profile of v3, /device:TPU:0, one launch (start us, length us, event | category | flops | bytes accessed | tf_op | source)
XLA Modules:
  0.0 20.0 jit_solution(7690830338422988246)
XLA Ops:
  0.0 18.7 %shard_map.64 = f32[16,32]{1,0:T(8,128)} custom-call(s32[2]{0:T(128)} %counts.1, bf16[2,256,6912]{2,1,0:T(8,128)(2,1)} %pre.1, bf16[2,256,2560]{2,1,0:T(8,128)(2,1)} %og.1, bf16[64,6912]{1,0:T(8,128)(2,1)} %bitcast.2, bf16[64,2560]{1,0:T(8,128)(2,1)} %bitcast.3, bf16[32,4096]{1,0:T(8,128)(2,1)} %q.1), custom_call_target="tpu_custom_call" | custom-call | flops 620756992 | bytes 9699328 | tf_op jit(solution)/shard_map/pallas_call | solution.py:222
  18.7 1.3 %copy.8 = f32[16,32]{1,0:T(8,128)} copy(f32[16,32]{1,0:T(8,128)} %shard_map.64) | data formatting | bytes 4096
